TPU v7x, 32 devices: a whole 2x2x4 slice. The times are simulated.
32 devices in a mesh: tm: 4 (over x, core), cols: 8 (over z, y).
Axes of the slice: x: 2, y: 2, z: 4, core: 2. Of those that a mesh axis runs over, the one named last changes fastest.
Arguments:
- inv_diag: bfloat16 [4, 2048, 2048], P('tm', 'cols'), as said below
- sub_diag: bfloat16 [4, 2048, 2048], P('tm', 'cols'), may hold values from -0.09375 to 0.09375
- rhs: bfloat16 [4, 2048, 4096], P('tm', None, 'cols'), may hold values from -6 to 6
- carry_in: bfloat16 [2048, 4096], P(None, 'cols'), may hold values from -6 to 6
Outputs:
- solved: float32 [4, 2048, 4096], P('tm', None, 'cols')
Inputs may be any that keep to these rules, and one draw needn't show every extreme that they name: Each block of inv_diag is lower triangular with diagonal entries between 0.5 and 1.5.
All inputs are finite; a program needn't handle non-finite values.
Results may differ from a plain program's by a relative error of at most 0.007.
Values may be sent and summed in bfloat16 or wider, within the bound.
A program may use at most 128 MiB of HBM per device.

v0:
```python
import functools

import jax
import jax.numpy as jnp
from jax import lax
from jax.experimental import pallas as pl
from jax.experimental.pallas import tpu as pltpu
from jax.sharding import PartitionSpec as P

MESH = pl.DeviceIdType.MESH
WIDE = 512
BATCH = 256
UP, DOWN, ACROSS = 0, 1, 2
TURN = 0


def kernel(sections, lines, inv_ref, sub_ref, rhs_ref, carry_ref, out_ref,
           factors, rhs, prior, update, solved, rounded,
           own_sem, load_sem, store_sem, send_sem, recv_sem, prior_send, prior_recv, turn_sem):
    section = lax.axis_index("tm")
    col = lax.axis_index("cols")
    z, y = col // 2, lax.rem(col, 2)
    rows = inv_ref.shape[1]
    order = inv_ref.shape[2]
    pieces = order // WIDE
    batches = rhs_ref.shape[2] // BATCH

    own_rows = pl.ds(pl.multiple_of(col * rows, rows), rows)
    own = [
        pltpu.make_async_copy(sub_ref.at[0], factors.at[0, own_rows, :], own_sem.at[0]),
        pltpu.make_async_copy(inv_ref.at[0], factors.at[1, own_rows, :], own_sem.at[1]),
    ]
    for copy in own:
        copy.start()
    loads = [pltpu.make_async_copy(rhs_ref.at[0], rhs, load_sem.at[0])]
    carries = [
        pltpu.make_async_copy(carry_ref.at[:, pl.ds(b * BATCH, BATCH)], prior.at[:, pl.ds(b * BATCH, BATCH)], load_sem.at[1 + b])
        for b in range(batches)
    ]

    barrier = pltpu.get_barrier_semaphore()

    def greet(cond, device):
        @pl.when(cond)
        def _():
            pl.semaphore_signal(barrier, inc=1, device_id=device, device_id_type=MESH)

    greet(z > 0, {"cols": col - 2})
    greet(z < lines - 1, {"cols": col + 2})
    pl.semaphore_signal(barrier, inc=1, device_id={"cols": 2 * z + 1 - y}, device_id_type=MESH)
    greet(section > 0, {"tm": section - 1})
    greet(section < sections - 1, {"tm": section + 1})
    ends = [z > 0, z < lines - 1, section > 0, section < sections - 1]
    pl.semaphore_wait(barrier, 1 + sum(jnp.where(end, 1, 0) for end in ends))

    def blocks(arr, z0):
        return pieces if arr == 0 else (z0 * 2 * rows) // WIDE + 1

    def piece(arr, z0, y0, j):
        c = 2 * z0 + y0
        return factors.at[arr, pl.ds(pl.multiple_of(c * rows, rows), rows),
                          pl.ds(pl.multiple_of(j * WIDE, WIDE), WIDE)]

    def remote(way, arr, z0, y0, j):
        c = 2 * z0 + y0
        ref = piece(arr, z0, y0, j)
        to = {UP: col + 2, DOWN: col - 2, ACROSS: 2 * z + 1 - y}[way]
        return pltpu.make_async_remote_copy(
            src_ref=ref, dst_ref=ref, send_sem=send_sem.at[way, arr, c, j],
            recv_sem=recv_sem.at[arr, c, j], device_id={"cols": to}, device_id_type=MESH)

    def if_(cond, fn):
        pl.when(cond)(fn)

    def each(count, fn):
        def body(j, carry):
            fn(j)
            return carry
        lax.fori_loop(0, count, body, 0)

    last = pieces - 1
    early = 2 * rows == WIDE and sections > 2

    def nth(arr, j):
        return lax.rem(j + last, pieces) if arr == 0 else j

    def along(arr, act, arrive, z0, y0, j, up, down):
        arrive(arr, z0, y0, j)
        if up:
            if_(z < lines - 1, lambda: act(remote(UP, arr, z0, y0, j)))
        if down:
            if_(z > 0, lambda: act(remote(DOWN, arr, z0, y0, j)))

    def line(arr, act, arrive, between=lambda d: None):
        def own_piece(k):
            j = nth(arr, k)
            act(remote(ACROSS, arr, z, y, j))
            along(arr, act, lambda *_: None, z, y, j, True, True)
        each(blocks(arr, z), own_piece)
        if arr == 0:
            along(arr, act, arrive, z, 1 - y, last, True, True)
        between(0)

        def from_side(z0, up):
            def one(k):
                j = nth(arr, k)
                along(arr, act, arrive, z0, y, j, up, not up)
                if arr == 0:
                    if_(j != last, lambda: act(remote(ACROSS, arr, z0, y, j)))
                else:
                    act(remote(ACROSS, arr, z0, y, j))
            each(blocks(arr, z0), one)
            if arr == 0:
                along(arr, act, arrive, z0, 1 - y, last, up, not up)

        def hop(d, carry):
            if_(z - d >= 0, lambda: from_side(z - d, True))
            if_(z + d < lines, lambda: from_side(z + d, False))
            return carry

        if early:
            for d in range(1, lines):
                hop(d, 0)
                between(d)
        else:
            lax.fori_loop(1, lines, hop, 0)

    def received(arr, z0, y0, j):
        remote(ACROSS, arr, z0, y0, j).wait_recv()

    def across(arr):
        def from_line(z0, carry):
            each(last if arr == 0 else blocks(arr, z0), lambda j: received(arr, z0, 1 - y, j))
            return carry
        lax.fori_loop(0, lines, from_line, 0)

    def rows_of(i):
        return pl.ds(i * WIDE if isinstance(i, int) else pl.multiple_of(i * WIDE, WIDE), WIDE)

    def handed(b, i):
        ref = (rows_of(i), pl.ds(b * BATCH, BATCH))
        return pltpu.make_async_remote_copy(
            src_ref=rounded.at[ref], dst_ref=prior.at[ref],
            send_sem=prior_send.at[b, i], recv_sem=prior_recv.at[b, i],
            device_id={"tm": section + 1}, device_id_type=MESH)

    def stored(b, i):
        ref = (pl.ds(i * WIDE, WIDE), pl.ds(b * BATCH, BATCH))
        return pltpu.make_async_copy(solved.at[ref], out_ref.at[0].at[ref], store_sem.at[b, i])

    def couple(i, cols):
        span = pl.ds(i * WIDE, WIDE)
        coupled = jnp.dot(factors[0, span, :], prior[:, cols], preferred_element_type=jnp.float32)
        update[span, cols] = (rhs[span, cols].astype(jnp.float32) - coupled).astype(jnp.bfloat16)

    def solve(i, cols, parts):
        span = pl.ds(i * WIDE, WIDE)
        known = (i + 1) * WIDE
        result = jnp.dot(factors[1, span, :known], update[:known, cols], preferred_element_type=jnp.float32)
        rounded[span, cols] = result.astype(jnp.bfloat16)
        for b in parts:
            if_(section < sections - 1, lambda: handed(b, i).start())
        solved[span, cols] = result
        for b in parts:
            stored(b, i).start()

    whole = pl.ds(0, batches * BATCH)

    def solve_plane(z0):
        for i in range(pieces):
            @pl.when(z0 == i)
            def _():
                for j in range(i + 1):
                    received(1, i, 1 - y, j)
                solve(i, whole, range(batches))

    def between(d):
        @pl.when(section < 2)
        def _():
            if d == 0:
                @pl.when(section == 1)
                def _():
                    for b in range(batches):
                        for i in range(pieces):
                            handed(b, i).wait_recv()
                for i in range(pieces // 2):
                    couple(i, whole)
            elif d == 1:
                for i in range(pieces // 2, pieces):
                    couple(i, whole)
            elif d == 2:
                solve_plane(z)
            else:
                solve_plane(z - d + 2)
                solve_plane(z + d - 2)
        if d == TURN:
            @pl.when(section == 0)
            def _():
                pl.semaphore_signal(turn_sem, inc=1, device_id={"tm": section + 1}, device_id_type=MESH)

    own[0].wait()
    loads[0].start()

    @pl.when(section == 0)
    def _():
        for copy in carries:
            copy.start()
    if early:
        @pl.when(section == 1)
        def _():
            pl.semaphore_wait(turn_sem, 1)
    line(0, lambda copy: copy.start(), received)
    own[1].wait()
    loads[0].wait()

    @pl.when(section == 0)
    def _():
        for copy in carries:
            copy.wait()

    if early:
        def between_all(d):
            if d == 0:
                across(0)
            between(d)
        line(1, lambda copy: copy.start(), received, between_all)

        @pl.when(section < 2)
        def _():
            for d in (lines - 2, lines - 1):
                solve_plane(z - d)
                solve_plane(z + d)
    else:
        line(1, lambda copy: copy.start(), received)
        across(0)

    @pl.when(section >= (2 if early else 0))
    def _():
        across(1)
        solved[...] = rhs[...].astype(jnp.float32)

        def add_group(g):
            @pl.when(section > 0)
            def _():
                for b in range(batches):
                    handed(b, g).wait_recv()
            group = pl.ds(pl.multiple_of(g * WIDE, WIDE), WIDE)
            for i in range(pieces):
                span = pl.ds(i * WIDE, WIDE)
                solved[span, :] -= jnp.dot(
                    factors[0, span, group], prior[group, :], preferred_element_type=jnp.float32)

        if early:
            first = jnp.where(section == 2, z, 0)
            add_group(first)

            def next_groups(d, carry):
                if_(first - d >= 0, lambda: add_group(first - d))
                if_(first + d < lines, lambda: add_group(first + d))
                return carry
            lax.fori_loop(1, lines, next_groups, 0)
        else:
            lax.fori_loop(0, pieces, lambda g, carry: (add_group(g), carry)[1], 0)
        for i in range(pieces):
            span = pl.ds(i * WIDE, WIDE)
            update[span, :] = solved[span, :].astype(jnp.bfloat16)
            solve(i, whole, range(batches))

    for arr in range(2):
        line(arr, lambda copy: copy.wait_send(), lambda *_: None)
    for b in range(batches):
        for i in range(pieces):
            stored(b, i).wait()
            if_(section < sections - 1, lambda: handed(b, i).wait_send())


def shards(sections, cols, inv_diag, sub_diag, rhs, carry_in):
    order, samples = carry_in.shape
    batches, pieces = samples // BATCH, order // WIDE
    flops = 4 * order * order * samples
    return pl.pallas_call(
        functools.partial(kernel, sections, cols // 2),
        out_shape=jax.ShapeDtypeStruct(rhs.shape, jnp.float32),
        in_specs=[pl.BlockSpec(memory_space=pl.ANY)] * 4,
        out_specs=pl.BlockSpec(memory_space=pl.ANY),
        scratch_shapes=[
            pltpu.VMEM((2, order, order), jnp.bfloat16),
            pltpu.VMEM((order, samples), jnp.bfloat16),
            pltpu.VMEM((order, samples), jnp.bfloat16),
            pltpu.VMEM((order, samples), jnp.bfloat16),
            pltpu.VMEM((order, samples), jnp.float32),
            pltpu.VMEM((order, samples), jnp.bfloat16),
            pltpu.SemaphoreType.DMA((2,)),
            pltpu.SemaphoreType.DMA((1 + batches,)),
            pltpu.SemaphoreType.DMA((batches, pieces)),
            pltpu.SemaphoreType.DMA((3, 2, cols, pieces)),
            pltpu.SemaphoreType.DMA((2, cols, pieces)),
            pltpu.SemaphoreType.DMA((batches, pieces)),
            pltpu.SemaphoreType.DMA((batches, pieces)),
            pltpu.SemaphoreType.REGULAR,
        ],
        compiler_params=pltpu.CompilerParams(
            collective_id=0, has_side_effects=True, vmem_limit_bytes=48 * 1024 * 1024),
        cost_estimate=pl.CostEstimate(flops=flops, bytes_accessed=10 * order * samples, transcendentals=0),
    )(inv_diag, sub_diag, rhs, carry_in)


def solution(mesh):
    in_specs = (
        P("tm", "cols", None),
        P("tm", "cols", None),
        P("tm", None, "cols"),
        P(None, "cols"),
    )
    out_specs = P("tm", None, "cols")
    body = functools.partial(shards, mesh.shape["tm"], mesh.shape["cols"])
    return jax.shard_map(body, mesh=mesh, in_specs=in_specs, out_specs=out_specs, check_vma=False)
```

profile of v0, /device:TPU:3, one launch (start us, length us, event | category | flops | bytes accessed | tf_op | source)
XLA Modules:
  0.0 185.9 jit_solution(12300435100097564528)
XLA Ops:
  0.0 0.0 copy-start
  0.0 1.6 copy-done
  1.6 0.0 copy-start.1
  1.6 1.2 copy-done.1
  2.8 0.0 copy-start.2
  2.8 1.2 copy-done.2
  4.0 177.2 %shard_map.46 = f32[1,2048,512]{2,1,0:T(8,128)} custom-call(bf16[1,256,2048]{2,1,0:T(8,128)(2,1)S(1)} %copy-done.1, bf16[1,256,2048]{2,1,0:T(8,128)(2,1)S(1)} %copy-done.2, bf16[1,2048,512]{2,1,0:T(8,128)(2,1)S(1)} %copy-done, bf16[2048,512]{1,0:T(8,128)(2,1)} %carry_ref.1), custom_call_target="tpu_custom_call" | custom-call | flops 8589934592 | bytes 10485760 | tf_op jit(solution)/shard_map/pallas_call | solution.py:281
  181.3 4.6 %copy.6 = f32[1,2048,512]{2,1,0:T(8,128)} copy(f32[1,2048,512]{2,1,0:T(8,128)} %shard_map.46) | data formatting | bytes 8388608
Async XLA Ops:
  0.0 1.6 copy-start
  1.6 1.2 copy-start.1
  2.8 1.2 copy-start.2
where the time goes:
time: 186 us
  Pallas kernels  177 us (95%)
  local copies, waits for them, and re-layouts  8.68 us (5%)
    pallas_call x1, Pallas kernels, shards(): pl.pallas_call(functools.partial(kernel, sections, cols // 2), out_shape=...  177 us
    unnamed x7, local copies, waits for them, and re-layouts  8.68 us

commit v1 on v0

v1 whole, which is shorter than its diff:
```python
import functools

import jax
import jax.numpy as jnp
from jax import lax
from jax.experimental import pallas as pl
from jax.experimental.pallas import tpu as pltpu
from jax.sharding import PartitionSpec as P

MESH = pl.DeviceIdType.MESH
WIDE = 512
UP, DOWN, ACROSS, PAIR = 0, 1, 2, 3


def kernel(stages, lines, inv_ref, sub_ref, rhs_ref, carry_ref, out_ref,
           factors, rhs, prior, update, middle, last, solved,
           own_sem, give_send, give_recv, rhs_sem, carry_sem,
           send_sem, recv_sem, pair_sem, store_sem, out_send, out_recv, prior_send, prior_recv):
    section = lax.axis_index("tm")
    col = lax.axis_index("cols")
    stage, core = section // 2, lax.rem(section, 2)
    z, y = col // 2, lax.rem(col, 2)
    rows, order = inv_ref.shape[1], inv_ref.shape[2]
    half = rhs_ref.shape[2] // 2
    part, plane, pieces = rows // 2, 2 * rows, order // WIDE
    sibling = {"tm": 2 * stage + 1 - core}

    def if_(cond, fn):
        pl.when(cond)(fn)

    def each(count, fn):
        def body(j, carry):
            fn(j)
            return carry
        lax.fori_loop(0, count, body, 0)

    mine = pl.ds(pl.multiple_of(col * rows, rows), rows)

    def own(arr):
        return pltpu.make_async_copy((sub_ref, inv_ref)[arr].at[0], factors.at[2 * core + arr, mine, :], own_sem.at[arr])

    def given(arr, owner):
        return pltpu.make_async_remote_copy(
            src_ref=(sub_ref, inv_ref)[arr].at[0], dst_ref=factors.at[2 * owner + arr, mine, :],
            send_sem=give_send.at[arr], recv_sem=give_recv.at[arr], device_id=sibling, device_id_type=MESH)

    def half_of(c):
        return pl.ds(pl.multiple_of(c * half, half), half)

    own_rhs = pltpu.make_async_copy(rhs_ref.at[0, :, half_of(core)], rhs.at[core], rhs_sem)

    def given_rhs(owner):
        return pltpu.make_async_remote_copy(
            src_ref=rhs_ref.at[0, :, half_of(1 - core)], dst_ref=rhs.at[owner],
            send_sem=give_send.at[2], recv_sem=give_recv.at[2], device_id=sibling, device_id_type=MESH)

    own_carry = pltpu.make_async_copy(carry_ref.at[:, half_of(core)], prior, carry_sem)

    own(0).start()
    own(1).start()

    barrier = pltpu.get_barrier_semaphore()

    def greet(cond, device):
        @pl.when(cond)
        def _():
            pl.semaphore_signal(barrier, inc=1, device_id=device, device_id_type=MESH)

    greet(z > 0, {"cols": col - 2})
    greet(z < lines - 1, {"cols": col + 2})
    pl.semaphore_signal(barrier, inc=1, device_id={"cols": 2 * z + 1 - y}, device_id_type=MESH)
    pl.semaphore_signal(barrier, inc=1, device_id=sibling, device_id_type=MESH)
    greet(stage > 0, {"tm": section - 2})
    greet(stage < stages - 1, {"tm": section + 2})
    ends = [z > 0, z < lines - 1, stage > 0, stage < stages - 1]
    pl.semaphore_wait(barrier, 2 + sum(jnp.where(end, 1, 0) for end in ends))

    given(0, core).start()
    given(1, core).start()
    own_rhs.start()
    given_rhs(core).start()
    if_(stage == 0, own_carry.start)

    def blocks(s, z0):
        return pieces if s % 2 == 0 else (z0 * plane) // WIDE + 1

    def nth(s, k):
        return lax.rem(k + pieces - 1, pieces) if s % 2 == 0 else k

    def turned(s, y0):
        return False if s % 2 == 1 else (True if s == 0 else y0 == 1)

    def piece(s, c, j, h):
        return factors.at[s, pl.ds(pl.multiple_of(c * rows + h * part, part), part),
                          pl.ds(pl.multiple_of(j * WIDE, WIDE), WIDE)]

    def hop(way, s, c, j):
        ref = piece(s, c, j, core)
        to = ({"cols": col + 2}, {"cols": col - 2}, {"cols": 2 * z + 1 - y}, sibling)[way]
        return pltpu.make_async_remote_copy(
            src_ref=ref, dst_ref=ref, send_sem=send_sem.at[way, s, c, j],
            recv_sem=pair_sem.at[s, c, j] if way == PAIR else recv_sem.at[s, c, j], device_id=to, device_id_type=MESH)

    def paired(s, c, j):
        ref = piece(s, c, j, 1 - core)
        return pltpu.make_async_remote_copy(
            src_ref=ref, dst_ref=ref, send_sem=send_sem.at[PAIR, s, c, j],
            recv_sem=pair_sem.at[s, c, j], device_id=sibling, device_id_type=MESH)

    def along(act, s, c, j, up, down):
        if up:
            if_(z < lines - 1, lambda: act(hop(UP, s, c, j)))
        if down:
            if_(z > 0, lambda: act(hop(DOWN, s, c, j)))

    def sides(d, fn):
        if_(z - d >= 0, lambda: fn(z - d, True))
        if_(z + d < lines, lambda: fn(z + d, False))

    def own_sends(s, act):
        def one(k):
            j = nth(s, k)
            act(hop(ACROSS, s, col, j))
            along(act, s, col, j, True, True)
        each(blocks(s, z), one)

    def turn(s, act, arrive):
        c = 2 * z + 1 - y
        if s % 2 == 0:
            def one():
                arrive(s, c, pieces - 1)
                along(act, s, c, pieces - 1, True, True)
                act(hop(PAIR, s, c, pieces - 1))
            if_(turned(s, 1 - y), one)

    def relay(s, d, act, arrive):
        def from_side(z0, up):
            c = 2 * z0 + y

            def one(k):
                j = nth(s, k)
                arrive(s, c, j)
                along(act, s, c, j, up, not up)
                if s % 2 == 1:
                    act(hop(ACROSS, s, c, j))
                else:
                    if_(jnp.logical_or(j < pieces - 1, jnp.logical_not(turned(s, y))), lambda: act(hop(ACROSS, s, c, j)))
                act(hop(PAIR, s, c, j))
            each(blocks(s, z0), one)
            if s % 2 == 0:
                def far_one():
                    arrive(s, c + 1 - 2 * y, pieces - 1)
                    along(act, s, c + 1 - 2 * y, pieces - 1, up, not up)
                    act(hop(PAIR, s, c + 1 - 2 * y, pieces - 1))
                if_(turned(s, 1 - y), far_one)
        sides(d, from_side)

    def far(s, z0, act, arrive):
        c = 2 * z0 + 1 - y

        def one(k):
            arrive(s, c, k)
            act(hop(PAIR, s, c, k))
        if s % 2 == 0:
            each(pieces - jnp.where(turned(s, 1 - y), 1, 0), one)
        else:
            each(blocks(s, z0), one)

    def whole(s, z0):
        def wait(c):
            each(blocks(s, z0), lambda j: paired(s, c, j).wait_recv())
        if_(z0 != z, lambda: wait(2 * z0 + y))
        wait(2 * z0 + 1 - y)

    def span_of(i):
        return pl.ds(i * plane if isinstance(i, int) else pl.multiple_of(i * plane, plane), plane)

    def handed(i):
        return pltpu.make_async_remote_copy(
            src_ref=last.at[span_of(i), :], dst_ref=prior.at[span_of(i), :],
            send_sem=prior_send.at[i], recv_sem=prior_recv.at[i],
            device_id={"tm": section + 2}, device_id_type=MESH)

    def stored(l, i):
        return pltpu.make_async_copy(
            solved.at[l, span_of(i), :], out_ref.at[0, span_of(i), half_of(core)], store_sem.at[i])

    def passed(l, i):
        return pltpu.make_async_remote_copy(
            src_ref=solved.at[l, span_of(i), :], dst_ref=out_ref.at[0, span_of(i), half_of(core)],
            send_sem=out_send.at[i], recv_sem=out_recv.at[i], device_id=sibling, device_id_type=MESH)

    def couple(l, i):
        span = span_of(i)
        coupled = jnp.dot(factors[2 * l, span, :], (prior, middle)[l][...], preferred_element_type=jnp.float32)
        update[span, :] = (rhs[l, span, :].astype(jnp.float32) - coupled).astype(jnp.bfloat16)

    def solve(l, z0):
        def one(i):
            span = span_of(i)
            known = ((i * plane) // WIDE + 1) * WIDE
            result = jnp.dot(factors[2 * l + 1, span, :known], update[:known, :], preferred_element_type=jnp.float32)
            (middle, last)[l][span, :] = result.astype(jnp.bfloat16)
            if l == 1:
                if_(stage < stages - 1, lambda: handed(i).start())
            solved[l, span, :] = result
            if_(core == l, lambda: stored(l, i).start())
            if_(core != l, lambda: passed(l, i).start())
        if isinstance(z0, int):
            one(z0)
        else:
            for i in range(lines):
                if_(z0 == i, lambda i=i: one(i))

    start = lambda copy: copy.start()
    arrived = lambda s, c, j: hop(ACROSS, s, c, j).wait_recv()

    def ready(s):
        l, arr = divmod(s, 2)
        if_(core == l, lambda: own(arr).wait())
        if_(core != l, lambda: given(arr, 1 - core).wait_recv())

    def begin(s):
        ready(s)
        own_sends(s, start)
        turn(s, start, arrived)

    def work(s, z0):
        far(s, z0, start, arrived)

        @pl.when(stage == 0)
        def _():
            whole(s, z0)
            (couple, solve)[s % 2](s // 2, z0)

    begin(0)
    own_rhs.wait()
    given_rhs(1 - core).wait_recv()
    if_(stage == 0, own_carry.wait)
    for s in range(4):
        def step(d, carry, s=s):
            relay(s, d, start, arrived)

            def side(k, carry):
                z0 = jnp.where(k == 0, z - d + 1, z + d - 1)
                if_(jnp.logical_and(jnp.logical_and(z0 >= 0, z0 < lines), jnp.logical_or(d > 1, k == 0)), lambda: work(s, z0))
                return carry
            lax.fori_loop(0, 2, side, 0)

            @pl.when(d == lines - 1)
            def _():
                if s < 3:
                    begin(s + 1)

            return carry
        lax.fori_loop(1, lines, step, 0)

        def end(k, carry, s=s):
            z0 = jnp.where(k == 0, z - lines + 1, z + lines - 1)
            if_(jnp.logical_and(z0 >= 0, z0 < lines), lambda: work(s, z0))
            return carry
        lax.fori_loop(0, 2, end, 0)

    @pl.when(stage > 0)
    def _():
        def all_whole(s):
            each(lines, lambda z0: whole(s, z0))

        def add(k):
            handed(k).wait_recv()
            group = pl.ds(pl.multiple_of(k * plane, plane), plane)
            for i in range(pieces):
                span = pl.ds(i * WIDE, WIDE)
                solved[1, span, :] -= jnp.dot(factors[0, span, group], prior[group, :], preferred_element_type=jnp.float32)

        for s in range(4):
            all_whole(s)
        solved[1] = rhs[0].astype(jnp.float32)

        def adds(d, carry):
            def side(k, carry):
                z0 = jnp.where(k == 0, z - d, z + d)
                if_(jnp.logical_and(jnp.logical_and(z0 >= 0, z0 < lines), jnp.logical_or(d > 0, k == 0)), lambda: add(z0))
                return carry
            return lax.fori_loop(0, 2, side, carry)
        lax.fori_loop(0, lines, adds, 0)
        update[...] = solved[1].astype(jnp.bfloat16)
        for i in range(lines):
            solve(0, i)
        for i in range(lines):
            couple(1, i)
        for i in range(lines):
            solve(1, i)

    sent = lambda copy: copy.wait_send()
    none = lambda *_: None
    for s in range(4):
        own_sends(s, sent)
        turn(s, sent, none)
        lax.fori_loop(1, lines, lambda d, carry, s=s: (relay(s, d, sent, none), carry)[1], 0)
        each(lines, lambda z0, s=s: far(s, z0, sent, none))
    for arr in range(2):
        given(arr, core).wait_send()
    given_rhs(core).wait_send()

    def finish(i):
        for l in range(2):
            if_(core == l, lambda l=l: stored(l, i).wait())
            if_(core != l, lambda l=l: passed(l, i).wait())
        if_(stage < stages - 1, lambda: handed(i).wait_send())
    each(lines, finish)


def shards(stages, cols, inv_diag, sub_diag, rhs, carry_in):
    order, samples = carry_in.shape
    half, lines, pieces = samples // 2, cols // 2, order // WIDE
    flops = 4 * order * order * samples
    return pl.pallas_call(
        functools.partial(kernel, stages, lines),
        out_shape=jax.ShapeDtypeStruct(rhs.shape, jnp.float32),
        in_specs=[pl.BlockSpec(memory_space=pl.ANY)] * 4,
        out_specs=pl.BlockSpec(memory_space=pl.ANY),
        scratch_shapes=[
            pltpu.VMEM((4, order, order), jnp.bfloat16),
            pltpu.VMEM((2, order, half), jnp.bfloat16),
            pltpu.VMEM((order, half), jnp.bfloat16),
            pltpu.VMEM((order, half), jnp.bfloat16),
            pltpu.VMEM((order, half), jnp.bfloat16),
            pltpu.VMEM((order, half), jnp.bfloat16),
            pltpu.VMEM((2, order, half), jnp.float32),
            pltpu.SemaphoreType.DMA((2,)),
            pltpu.SemaphoreType.DMA((3,)),
            pltpu.SemaphoreType.DMA((3,)),
            pltpu.SemaphoreType.DMA,
            pltpu.SemaphoreType.DMA,
            pltpu.SemaphoreType.DMA((4, 4, cols, pieces)),
            pltpu.SemaphoreType.DMA((4, cols, pieces)),
            pltpu.SemaphoreType.DMA((4, cols, pieces)),
            pltpu.SemaphoreType.DMA((lines,)),
            pltpu.SemaphoreType.DMA((lines,)),
            pltpu.SemaphoreType.DMA((lines,)),
            pltpu.SemaphoreType.DMA((lines,)),
            pltpu.SemaphoreType.DMA((lines,)),
        ],
        compiler_params=pltpu.CompilerParams(
            collective_id=0, has_side_effects=True, vmem_limit_bytes=60 * 1024 * 1024),
        cost_estimate=pl.CostEstimate(flops=flops, bytes_accessed=10 * order * samples, transcendentals=0),
    )(inv_diag, sub_diag, rhs, carry_in)


def solution(mesh):
    in_specs = (
        P("tm", "cols", None),
        P("tm", "cols", None),
        P("tm", None, "cols"),
        P(None, "cols"),
    )
    out_specs = P("tm", None, "cols")
    body = functools.partial(shards, mesh.shape["tm"] // 2, mesh.shape["cols"])
    return jax.shard_map(body, mesh=mesh, in_specs=in_specs, out_specs=out_specs, check_vma=False)
```

time: 186 us -> 192 us (1.032)
  Pallas kernels: 177 us -> 187 us
  local copies, waits for them, and re-layouts: 8.68 us -> 4.64 us
    pallas_call x1, Pallas kernels: 177 us -> 187 us  [shards(): pl.pallas_call(functools.partial(kernel, stages, lines), out_shape=jax.Sh...]
    unnamed x7 -> x1, local copies, waits for them, and re-layouts: 8.68 us -> 4.64 us
where the time goes in v1:
time: 192 us; the launch traced here: 191 us
  Pallas kernels  187 us (97%)
  local copies, waits for them, and re-layouts  4.64 us (2%)
    pallas_call x1, Pallas kernels, shards(): pl.pallas_call(functools.partial(kernel, stages, lines), out_shape=jax.Sh...  187 us
    unnamed x1, local copies, waits for them, and re-layouts  4.64 us

profile of v1, /device:TPU:3, one launch (start us, length us, event | category | flops | bytes accessed | tf_op | source)
XLA Modules:
  0.0 191.5 jit_solution(15383651124176153378)
XLA Ops:
  0.0 186.8 %shard_map.46 = f32[1,2048,512]{2,1,0:T(8,128)} custom-call(bf16[1,256,2048]{2,1,0:T(8,128)(2,1)} %inv_ref.1, bf16[1,256,2048]{2,1,0:T(8,128)(2,1)} %sub_ref.1, bf16[1,2048,512]{2,1,0:T(8,128)(2,1)} %rhs_ref.1, bf16[2048,512]{1,0:T(8,128)(2,1)} %carry_ref.1), custom_call_target="tpu_custom_call" | custom-call | flops 8589934592 | bytes 10485760 | tf_op jit(solution)/shard_map/pallas_call | solution.py:318
  186.9 4.6 %copy.6 = f32[1,2048,512]{2,1,0:T(8,128)} copy(f32[1,2048,512]{2,1,0:T(8,128)} %shard_map.46) | data formatting | bytes 8388608

commit v2 on v1

v2 whole, which is shorter than its diff:
```python
import functools

import jax
import jax.numpy as jnp
from jax import lax
from jax.experimental import pallas as pl
from jax.experimental.pallas import tpu as pltpu
from jax.sharding import PartitionSpec as P

MESH = pl.DeviceIdType.MESH
WIDE = 512
UP, DOWN, ACROSS, PAIR = 0, 1, 2, 3
LAG = 3
LAGM = 4
LATE = 7
LATER = 1


def kernel(stages, lines, inv_ref, sub_ref, rhs_ref, carry_ref, out_ref,
           factors, rhs, prior, update, staged,
           own_sem, give_send, give_recv, rhs_sem, carry_sem,
           send_sem, recv_sem, pair_sem, store_sem, out_send, out_recv, prior_send, prior_recv):
    section = lax.axis_index("tm")
    col = lax.axis_index("cols")
    stage, core = section // 2, lax.rem(section, 2)
    z, y = col // 2, lax.rem(col, 2)
    rows, order = inv_ref.shape[1], inv_ref.shape[2]
    half = rhs_ref.shape[2] // 2
    plane, pieces = 2 * rows, order // WIDE
    narrow = WIDE // 2
    sibling = {"tm": 2 * stage + 1 - core}

    def if_(cond, fn):
        pl.when(cond)(fn)

    def each(count, fn):
        def body(j, carry):
            fn(j)
            return carry
        lax.fori_loop(0, count, body, 0)

    mine = pl.ds(pl.multiple_of(col * rows, rows), rows)

    def own(arr):
        return pltpu.make_async_copy((sub_ref, inv_ref)[arr].at[0], factors.at[2 * core + arr, mine, :], own_sem.at[arr])

    def given(arr, owner):
        return pltpu.make_async_remote_copy(
            src_ref=(sub_ref, inv_ref)[arr].at[0], dst_ref=factors.at[2 * owner + arr, mine, :],
            send_sem=give_send.at[arr], recv_sem=give_recv.at[arr], device_id=sibling, device_id_type=MESH)

    def half_of(c):
        return pl.ds(pl.multiple_of(c * half, half), half)

    own_rhs = pltpu.make_async_copy(rhs_ref.at[0, :, half_of(core)], rhs.at[core], rhs_sem)

    def given_rhs(owner):
        return pltpu.make_async_remote_copy(
            src_ref=rhs_ref.at[0, :, half_of(1 - core)], dst_ref=rhs.at[owner],
            send_sem=give_send.at[2], recv_sem=give_recv.at[2], device_id=sibling, device_id_type=MESH)

    own_carry = pltpu.make_async_copy(carry_ref.at[:, half_of(core)], prior.at[0], carry_sem)

    own(0).start()
    own(1).start()

    barrier = pltpu.get_barrier_semaphore()

    def greet(cond, device):
        @pl.when(cond)
        def _():
            pl.semaphore_signal(barrier, inc=1, device_id=device, device_id_type=MESH)

    greet(z > 0, {"cols": col - 2})
    greet(z < lines - 1, {"cols": col + 2})
    pl.semaphore_signal(barrier, inc=1, device_id={"cols": 2 * z + 1 - y}, device_id_type=MESH)
    pl.semaphore_signal(barrier, inc=1, device_id=sibling, device_id_type=MESH)
    greet(stage > 0, {"tm": section - 2})
    greet(stage < stages - 1, {"tm": section + 2})
    ends = [z > 0, z < lines - 1, stage > 0, stage < stages - 1]
    pl.semaphore_wait(barrier, 2 + sum(jnp.where(end, 1, 0) for end in ends))

    given(0, core).start()
    given(1, core).start()
    own_rhs.start()
    given_rhs(core).start()
    if_(stage == 0, own_carry.start)

    first = stage == 0

    def even(s):
        return lax.rem(s, 2) == 0

    def blocks(s, c):
        return jnp.where(even(s), pieces, (c * rows) // WIDE + 1)

    def turns(s, c):
        return jnp.where(s == 0, 1, jnp.where(s == 2, lax.rem(c, 2), 0))

    def nth(s, c, k):
        return lax.rem(k + blocks(s, c) - turns(s, c), blocks(s, c))

    def hop(way, s, c, j, wide):
        ref = factors.at[s, pl.ds(pl.multiple_of(c * rows, rows), rows), pl.ds(pl.multiple_of(j * WIDE, WIDE), wide)]
        to = ({"tm": 2 * stage, "cols": col + 2}, {"tm": 2 * stage + 1, "cols": col - 2}, {"cols": 2 * z + 1 - y}, sibling)[way]
        return pltpu.make_async_remote_copy(
            src_ref=ref, dst_ref=ref, send_sem=send_sem.at[way, s, c, j],
            recv_sem=pair_sem.at[s, c, j] if way == PAIR else recv_sem.at[s, c, j], device_id=to, device_id_type=MESH)

    def mine_of(z0, j):
        return jnp.where(z0 == z, lax.rem(j, 2) == core, (core == 0) == (z0 < z))

    def cut(s, c, j):
        return jnp.logical_and(jnp.logical_not(even(s)), (c + 1) * rows <= j * WIDE + narrow)

    def by_width(s, c, j, fn):
        short = cut(s, c, j)
        if_(short, lambda: fn(narrow))
        if_(jnp.logical_not(short), lambda: fn(WIDE))

    def moves(act, s, c, j, up, down, across, pair, arrive):
        def fn(wide):
            if arrive:
                hop(ACROSS, s, c, j, wide).wait_recv()
            for way, cond in ((UP, up), (DOWN, down), (ACROSS, across), (PAIR, pair)):
                if cond is True:
                    act(hop(way, s, c, j, wide))
                elif cond is not False:
                    if_(cond, lambda way=way: act(hop(way, s, c, j, wide)))
        by_width(s, c, j, fn)

    can_up, can_down = z < lines - 1, z > 0
    up, down = jnp.logical_and(can_up, core == 0), jnp.logical_and(can_down, core == 1)

    def own_sends(s, act):
        def one(k):
            j = nth(s, col, k)
            across = jnp.logical_and(k >= turns(s, col), lax.rem(j, 2) == core)
            moves(act, s, col, j, up, down, across, False, False)
        each(blocks(s, col), one)

    def turning(act):
        def of(s):
            def one(k):
                j = nth(s, col, k)
                if_(lax.rem(j, 2) == core, lambda: moves(act, s, col, j, False, False, True, False, False))
            each(turns(s, col), one)
        each(4, of)

    def turn(s, act, arrive):
        c = 2 * z + 1 - y

        def one(k):
            j = nth(s, c, k)
            if_(lax.rem(j, 2) == core, lambda: moves(act, s, c, j, can_up, can_down, False, True, arrive))
        each(turns(s, c), one)

    def relay(s, d, act, arrive):
        z0 = jnp.where(core == 0, z - d, z + d)

        @pl.when(jnp.logical_and(z0 >= 0, z0 < lines))
        def _():
            near, across_from = 2 * z0 + y, 2 * z0 + 1 - y
            count = blocks(s, near)

            def one(i):
                is_far = i >= count
                c = jnp.where(is_far, across_from, near)
                j = nth(s, c, jnp.where(is_far, i - count, i))
                across = jnp.logical_and(jnp.logical_not(is_far), j < count - turns(s, near))
                moves(act, s, c, j, up, down, across, True, arrive)
            each(count + turns(s, across_from), one)

    def far(s, z0, act, arrive):
        c = 2 * z0 + 1 - y

        def one(j):
            if_(mine_of(z0, j), lambda: moves(act, s, c, j, False, False, False, True, arrive))
        each(blocks(s, c) - turns(s, c), one)

    def whole(s, z0):
        def wait(c):
            def one(j):
                if_(jnp.logical_not(mine_of(z0, j)), lambda: by_width(s, c, j, lambda wide: hop(PAIR, s, c, j, wide).wait_recv()))
            each(blocks(s, c), one)
        if_(z0 != z, lambda: wait(2 * z0 + y))
        wait(2 * z0 + 1 - y)

    def span_of(c):
        return pl.ds(c * rows if isinstance(c, int) else pl.multiple_of(c * rows, rows), rows)

    def handed(c):
        return pltpu.make_async_remote_copy(
            src_ref=prior.at[2, span_of(c), :], dst_ref=prior.at[0, span_of(c), :],
            send_sem=prior_send.at[c], recv_sem=prior_recv.at[c],
            device_id={"tm": section + 2}, device_id_type=MESH)

    def stored(l, c):
        return pltpu.make_async_copy(
            staged.at[l, span_of(c), :], out_ref.at[0, span_of(c), half_of(core)], store_sem.at[c])

    def passed(l, c, owner):
        return pltpu.make_async_remote_copy(
            src_ref=staged.at[l, span_of(c), :], dst_ref=out_ref.at[0, span_of(c), half_of(owner)],
            send_sem=out_send.at[c], recv_sem=out_recv.at[c], device_id=sibling, device_id_type=MESH)

    def couple(l, z0):
        span = pl.ds(pl.multiple_of(z0 * plane, plane), plane)
        coupled = jnp.dot(factors[2 * l, span, :], prior[l], preferred_element_type=jnp.float32)
        update[span, :] = (rhs[l, span, :].astype(jnp.float32) - coupled).astype(jnp.bfloat16)

    def solve(l, c):
        for i in range(2 * lines):
            @pl.when(c == i)
            def _(i=i):
                known = -(-(i + 1) * rows // narrow) * narrow
                result = jnp.dot(factors[2 * l + 1, span_of(i), :known], update[:known, :], preferred_element_type=jnp.float32)
                prior[l + 1, span_of(i), :] = result.astype(jnp.bfloat16)
                if_(jnp.logical_and(l == 1, stage < stages - 1), lambda: handed(i).start())
                staged[l, span_of(i), :] = result
                if_(core == l, lambda: stored(l, i).start())
                if_(core != l, lambda: passed(l, i, core).start())

    start = lambda copy: copy.start()

    def ready(s):
        l, arr = s // 2, lax.rem(s, 2)
        for a in range(2):
            if_(jnp.logical_and(core == l, arr == a), lambda a=a: own(a).wait())
            if_(jnp.logical_and(core != l, arr == a), lambda a=a: given(a, 1 - core).wait_recv())

    def fetch(s, z0):
        far(s, z0, start, True)

    def work(s, z0):
        @pl.when(first)
        def _():
            whole(s, z0)
            if_(even(s), lambda: couple(s // 2, z0))

            @pl.when(jnp.logical_not(even(s)))
            def _():
                lax.fori_loop(0, 2, lambda k, carry: (solve(s // 2, 2 * z0 + k), carry)[1], 0)

    each(4, ready)
    turning(start)
    own_sends(0, start)
    own_rhs.wait()
    given_rhs(1 - core).wait_recv()
    if_(first, own_carry.wait)

    steps = 4 * lines

    def in_order(d, fn):
        def side(k, carry):
            z0 = jnp.where(k == 0, z - d, z + d)
            if_(jnp.logical_and(jnp.logical_and(z0 >= 0, z0 < lines), jnp.logical_or(d > 0, k == 0)), lambda: fn(z0))
            return carry
        lax.fori_loop(0, 2, side, 0)

    def items(t, lag, fn):
        w = t - lag
        if_(jnp.logical_and(w >= 0, w < steps), lambda: in_order(lax.rem(w, lines), lambda z0: fn(w // lines, z0)))

    inside = jnp.logical_and(z > 0, z < lines - 1)
    lag = jnp.where(first, jnp.where(inside, LAGM, LAG), LATE)

    def step(t, carry):
        s, d = t // lines, lax.rem(t, lines)

        @pl.when(t < steps)
        def _():
            if_(d == 0, lambda: turn(s, start, True))
            if_(d > 0, lambda: relay(s, d, start, True))
            if_(jnp.logical_and(d == lines - 1, s < 3), lambda: own_sends(s + 1, start))
        items(t, lag, fetch)
        items(t, lag + LATER, work)
        return carry
    lax.fori_loop(0, steps + max(LAG, LAGM, LATE) + LATER, step, 0)

    @pl.when(stage > 0)
    def _():
        each(4, lambda s: each(lines, lambda z0: whole(s, z0)))
        staged[1] = rhs[0].astype(jnp.float32)

        def add(k):
            for c in range(2):
                handed(2 * k + c).wait_recv()
            group = pl.ds(pl.multiple_of(k * plane, plane), plane)
            for i in range(pieces):
                span = pl.ds(i * WIDE, WIDE)
                staged[1, span, :] -= jnp.dot(factors[0, span, group], prior[0, group, :], preferred_element_type=jnp.float32)
        each(lines, lambda d: in_order(d, add))
        update[...] = staged[1].astype(jnp.bfloat16)
        each(2 * lines, lambda c: solve(0, c))
        each(lines, lambda z0: couple(1, z0))
        each(2 * lines, lambda c: solve(1, c))

    sent = lambda copy: copy.wait_send()

    turning(sent)

    def sends(s):
        own_sends(s, sent)
        turn(s, sent, False)
        lax.fori_loop(1, lines, lambda d, carry: (relay(s, d, sent, False), carry)[1], 0)
        each(lines, lambda z0: far(s, z0, sent, False))
    each(4, sends)
    for arr in range(2):
        given(arr, core).wait_send()
    given_rhs(core).wait_send()

    def finish(c):
        for l in range(2):
            if_(core == l, lambda l=l: stored(l, c).wait())
            if_(core != l, lambda l=l: passed(l, c, core).wait_send())
        passed(0, c, 1 - core).wait_recv()
        if_(stage < stages - 1, lambda: handed(c).wait_send())
    each(2 * lines, finish)


def shards(stages, cols, inv_diag, sub_diag, rhs, carry_in):
    order, samples = carry_in.shape
    half, lines, pieces = samples // 2, cols // 2, order // WIDE
    flops = 4 * order * order * samples
    return pl.pallas_call(
        functools.partial(kernel, stages, lines),
        out_shape=jax.ShapeDtypeStruct(rhs.shape, jnp.float32),
        in_specs=[pl.BlockSpec(memory_space=pl.ANY)] * 4,
        out_specs=pl.BlockSpec(memory_space=pl.ANY),
        scratch_shapes=[
            pltpu.VMEM((4, order, order), jnp.bfloat16),
            pltpu.VMEM((2, order, half), jnp.bfloat16),
            pltpu.VMEM((3, order, half), jnp.bfloat16),
            pltpu.VMEM((order, half), jnp.bfloat16),
            pltpu.VMEM((2, order, half), jnp.float32),
            pltpu.SemaphoreType.DMA((2,)),
            pltpu.SemaphoreType.DMA((3,)),
            pltpu.SemaphoreType.DMA((3,)),
            pltpu.SemaphoreType.DMA,
            pltpu.SemaphoreType.DMA,
            pltpu.SemaphoreType.DMA((4, 4, cols, pieces)),
            pltpu.SemaphoreType.DMA((4, cols, pieces)),
            pltpu.SemaphoreType.DMA((4, cols, pieces)),
            pltpu.SemaphoreType.DMA((cols,)),
            pltpu.SemaphoreType.DMA((cols,)),
            pltpu.SemaphoreType.DMA((cols,)),
            pltpu.SemaphoreType.DMA((cols,)),
            pltpu.SemaphoreType.DMA((cols,)),
        ],
        compiler_params=pltpu.CompilerParams(
            collective_id=0, has_side_effects=True, vmem_limit_bytes=60 * 1024 * 1024),
        cost_estimate=pl.CostEstimate(flops=flops, bytes_accessed=10 * order * samples, transcendentals=0),
    )(inv_diag, sub_diag, rhs, carry_in)


def solution(mesh):
    in_specs = (
        P("tm", "cols", None),
        P("tm", "cols", None),
        P("tm", None, "cols"),
        P(None, "cols"),
    )
    out_specs = P("tm", None, "cols")
    body = functools.partial(shards, mesh.shape["tm"] // 2, mesh.shape["cols"])
    return jax.shard_map(body, mesh=mesh, in_specs=in_specs, out_specs=out_specs, check_vma=False)
```

time: 192 us -> 183 us (0.953)
  Pallas kernels: 187 us -> 178 us
    pallas_call x1, Pallas kernels: 187 us -> 178 us  [shards(): pl.pallas_call(functools.partial(kernel, stages, lines), out_shape=jax.Sh...]
where the time goes in v2:
time: 183 us; the launch traced here: 182 us
  Pallas kernels  178 us (97%)
  local copies, waits for them, and re-layouts  4.64 us (3%)
    pallas_call x1, Pallas kernels, shards(): pl.pallas_call(functools.partial(kernel, stages, lines), out_shape=jax.Sh...  178 us
    unnamed x1, local copies, waits for them, and re-layouts  4.64 us

profile of v2, /device:TPU:3, one launch (start us, length us, event | category | flops | bytes accessed | tf_op | source)
XLA Modules:
  0.0 182.5 jit_solution(9909287751389030718)
XLA Ops:
  0.0 177.8 %shard_map.46 = f32[1,2048,512]{2,1,0:T(8,128)} custom-call(bf16[1,256,2048]{2,1,0:T(8,128)(2,1)} %inv_ref.1, bf16[1,256,2048]{2,1,0:T(8,128)(2,1)} %sub_ref.1, bf16[1,2048,512]{2,1,0:T(8,128)(2,1)} %rhs_ref.1, bf16[2048,512]{1,0:T(8,128)(2,1)} %carry_ref.1), custom_call_target="tpu_custom_call" | custom-call | flops 8589934592 | bytes 10485760 | tf_op jit(solution)/shard_map/pallas_call | solution.py:326
  177.8 4.6 %copy.6 = f32[1,2048,512]{2,1,0:T(8,128)} copy(f32[1,2048,512]{2,1,0:T(8,128)} %shard_map.46) | data formatting | bytes 8388608

commit v3 on v2

--- a/solution.py
+++ b/solution.py
@@ -10,10 +10,14 @@
 MESH = pl.DeviceIdType.MESH
 WIDE = 512
 UP, DOWN, ACROSS, PAIR = 0, 1, 2, 3
-LAG = 3
+LAG = 4
 LAGM = 4
-LATE = 7
-LATER = 1
+LATE = 6
+AHEAD = 2
+LAST = 2
+END_LAG = 1
+BEHIND = 1
+TALL = 1024
 
 
 def kernel(stages, lines, inv_ref, sub_ref, rhs_ref, carry_ref, out_ref,
@@ -81,10 +85,6 @@
     pl.semaphore_wait(barrier, 2 + sum(jnp.where(end, 1, 0) for end in ends))
 
     given(0, core).start()
-    given(1, core).start()
-    own_rhs.start()
-    given_rhs(core).start()
-    if_(stage == 0, own_carry.start)
 
     first = stage == 0
 
@@ -107,8 +107,10 @@
             src_ref=ref, dst_ref=ref, send_sem=send_sem.at[way, s, c, j],
             recv_sem=pair_sem.at[s, c, j] if way == PAIR else recv_sem.at[s, c, j], device_id=to, device_id_type=MESH)
 
-    def mine_of(z0, j):
-        return jnp.where(z0 == z, lax.rem(j, 2) == core, (core == 0) == (z0 < z))
+    light = core == jnp.where(2 * z < lines, 0, 1)
+
+    def mine_of(z0):
+        return jnp.where(z0 == z, light, (core == 0) == (z0 < z))
 
     def cut(s, c, j):
         return jnp.logical_and(jnp.logical_not(even(s)), (c + 1) * rows <= j * WIDE + narrow)
@@ -135,25 +137,19 @@
     def own_sends(s, act):
         def one(k):
             j = nth(s, col, k)
-            across = jnp.logical_and(k >= turns(s, col), lax.rem(j, 2) == core)
+            across = jnp.logical_and(k >= turns(s, col), light)
             moves(act, s, col, j, up, down, across, False, False)
         each(blocks(s, col), one)
 
     def turning(act):
         def of(s):
-            def one(k):
-                j = nth(s, col, k)
-                if_(lax.rem(j, 2) == core, lambda: moves(act, s, col, j, False, False, True, False, False))
-            each(turns(s, col), one)
-        each(4, of)
+            if_(light, lambda: each(turns(s, col), lambda k: moves(act, s, col, nth(s, col, k), False, False, True, False, False)))
+        return of
 
     def turn(s, act, arrive):
         c = 2 * z + 1 - y
 
-        def one(k):
-            j = nth(s, c, k)
-            if_(lax.rem(j, 2) == core, lambda: moves(act, s, c, j, can_up, can_down, False, True, arrive))
-        each(turns(s, c), one)
+        if_(light, lambda: each(turns(s, c), lambda k: moves(act, s, c, nth(s, c, k), can_up, can_down, False, True, arrive)))
 
     def relay(s, d, act, arrive):
         z0 = jnp.where(core == 0, z - d, z + d)
@@ -175,13 +171,13 @@
         c = 2 * z0 + 1 - y
 
         def one(j):
-            if_(mine_of(z0, j), lambda: moves(act, s, c, j, False, False, False, True, arrive))
+            if_(mine_of(z0), lambda: moves(act, s, c, j, False, False, False, True, arrive))
         each(blocks(s, c) - turns(s, c), one)
 
     def whole(s, z0):
         def wait(c):
             def one(j):
-                if_(jnp.logical_not(mine_of(z0, j)), lambda: by_width(s, c, j, lambda wide: hop(PAIR, s, c, j, wide).wait_recv()))
+                if_(jnp.logical_not(mine_of(z0)), lambda: by_width(s, c, j, lambda wide: hop(PAIR, s, c, j, wide).wait_recv()))
             each(blocks(s, c), one)
         if_(z0 != z, lambda: wait(2 * z0 + y))
         wait(2 * z0 + 1 - y)
@@ -197,11 +193,11 @@
 
     def stored(l, c):
         return pltpu.make_async_copy(
-            staged.at[l, span_of(c), :], out_ref.at[0, span_of(c), half_of(core)], store_sem.at[c])
+            prior.at[l + 1, span_of(c), :], out_ref.at[0, span_of(c), half_of(core)], store_sem.at[c])
 
     def passed(l, c, owner):
         return pltpu.make_async_remote_copy(
-            src_ref=staged.at[l, span_of(c), :], dst_ref=out_ref.at[0, span_of(c), half_of(owner)],
+            src_ref=prior.at[l + 1, span_of(c), :], dst_ref=out_ref.at[0, span_of(c), half_of(owner)],
             send_sem=out_send.at[c], recv_sem=out_recv.at[c], device_id=sibling, device_id_type=MESH)
 
     def couple(l, z0):
@@ -209,17 +205,24 @@
         coupled = jnp.dot(factors[2 * l, span, :], prior[l], preferred_element_type=jnp.float32)
         update[span, :] = (rhs[l, span, :].astype(jnp.float32) - coupled).astype(jnp.bfloat16)
 
-    def solve(l, c):
-        for i in range(2 * lines):
-            @pl.when(c == i)
+    def solve(l, z0):
+        for i in range(lines):
+            @pl.when(z0 == i)
             def _(i=i):
-                known = -(-(i + 1) * rows // narrow) * narrow
-                result = jnp.dot(factors[2 * l + 1, span_of(i), :known], update[:known, :], preferred_element_type=jnp.float32)
-                prior[l + 1, span_of(i), :] = result.astype(jnp.bfloat16)
-                if_(jnp.logical_and(l == 1, stage < stages - 1), lambda: handed(i).start())
-                staged[l, span_of(i), :] = result
-                if_(core == l, lambda: stored(l, i).start())
-                if_(core != l, lambda: passed(l, i, core).start())
+                both, lower = slice(i * plane, (i + 1) * plane), slice(i * plane + rows, (i + 1) * plane)
+                known, rest = (-(-(2 * i + k) * rows // narrow) * narrow for k in (1, 2))
+                result = jnp.dot(factors[2 * l + 1, both, :known], update[:known, :], preferred_element_type=jnp.float32)
+                if rest > known:
+                    more = jnp.dot(factors[2 * l + 1, lower, known:rest], update[known:rest, :], preferred_element_type=jnp.float32)
+                    prior[l + 1, slice(i * plane, i * plane + rows), :] = result[:rows].astype(jnp.bfloat16)
+                    prior[l + 1, lower, :] = (result[rows:] + more).astype(jnp.bfloat16)
+                else:
+                    prior[l + 1, both, :] = result.astype(jnp.bfloat16)
+                for c in (2 * i, 2 * i + 1):
+                    if_(jnp.logical_and(l == 1, stage < stages - 1), lambda c=c: handed(c).start())
+                for c in (2 * i, 2 * i + 1):
+                    if_(core == l, lambda c=c: stored(l, c).start())
+                    if_(core != l, lambda c=c: passed(l, c, core).start())
 
     start = lambda copy: copy.start()
 
@@ -240,11 +243,19 @@
 
             @pl.when(jnp.logical_not(even(s)))
             def _():
-                lax.fori_loop(0, 2, lambda k, carry: (solve(s // 2, 2 * z0 + k), carry)[1], 0)
-
-    each(4, ready)
-    turning(start)
+                solve(s // 2, z0)
+
+    ready(0)
+    turning(start)(0)
     own_sends(0, start)
+    given(1, core).start()
+    if_(first, own_carry.start)
+    own_rhs.start()
+    given_rhs(core).start()
+    ready(2)
+    turning(start)(2)
+    ready(1)
+    ready(3)
     own_rhs.wait()
     given_rhs(1 - core).wait_recv()
     if_(first, own_carry.wait)
@@ -258,12 +269,20 @@
             return carry
         lax.fori_loop(0, 2, side, 0)
 
-    def items(t, lag, fn):
-        w = t - lag
-        if_(jnp.logical_and(w >= 0, w < steps), lambda: in_order(lax.rem(w, lines), lambda z0: fn(w // lines, z0)))
-
     inside = jnp.logical_and(z > 0, z < lines - 1)
     lag = jnp.where(first, jnp.where(inside, LAGM, LAG), LATE)
+    ending = jnp.where(jnp.logical_and(first, jnp.logical_not(inside)), steps - lines + LAST, steps + 99)
+
+    def due(t):
+        late = jnp.where(t >= ending, END_LAG, lag)
+        return jnp.clip(2 * (t - late), 0, 2 * steps + BEHIND)
+
+    def half_step(h, fn):
+        w, k = h // 2, lax.rem(h, 2)
+        s, d = w // lines, lax.rem(w, lines)
+        z0 = jnp.where(k == 0, z - d, z + d)
+        real = jnp.logical_and(jnp.logical_and(h >= 0, h < 2 * steps), jnp.logical_or(d > 0, k == 0))
+        if_(jnp.logical_and(real, jnp.logical_and(z0 >= 0, z0 < lines)), lambda: fn(s, z0))
 
     def step(t, carry):
         s, d = t // lines, lax.rem(t, lines)
@@ -272,16 +291,20 @@
         def _():
             if_(d == 0, lambda: turn(s, start, True))
             if_(d > 0, lambda: relay(s, d, start, True))
-            if_(jnp.logical_and(d == lines - 1, s < 3), lambda: own_sends(s + 1, start))
-        items(t, lag, fetch)
-        items(t, lag + LATER, work)
+            if_(jnp.logical_and(d == lines - AHEAD, s < 3), lambda: own_sends(s + 1, start))
+
+        def item(h, carry):
+            half_step(h, fetch)
+            half_step(h - BEHIND, work)
+            return carry
+        lax.fori_loop(due(t), due(t + 1), item, 0)
         return carry
-    lax.fori_loop(0, steps + max(LAG, LAGM, LATE) + LATER, step, 0)
+    lax.fori_loop(0, steps + max(LAG, LAGM, LATE) + BEHIND, step, 0)
 
     @pl.when(stage > 0)
     def _():
         each(4, lambda s: each(lines, lambda z0: whole(s, z0)))
-        staged[1] = rhs[0].astype(jnp.float32)
+        staged[...] = rhs[0].astype(jnp.float32)
 
         def add(k):
             for c in range(2):
@@ -289,16 +312,19 @@
             group = pl.ds(pl.multiple_of(k * plane, plane), plane)
             for i in range(pieces):
                 span = pl.ds(i * WIDE, WIDE)
-                staged[1, span, :] -= jnp.dot(factors[0, span, group], prior[0, group, :], preferred_element_type=jnp.float32)
+                staged[span, :] -= jnp.dot(factors[0, span, group], prior[0, group, :], preferred_element_type=jnp.float32)
         each(lines, lambda d: in_order(d, add))
-        update[...] = staged[1].astype(jnp.bfloat16)
-        each(2 * lines, lambda c: solve(0, c))
-        each(lines, lambda z0: couple(1, z0))
-        each(2 * lines, lambda c: solve(1, c))
+        update[...] = staged[...].astype(jnp.bfloat16)
+        each(lines, lambda z0: solve(0, z0))
+        for i in range(order // TALL):
+            span = slice(i * TALL, (i + 1) * TALL)
+            coupled = jnp.dot(factors[2, span, :], prior[1], preferred_element_type=jnp.float32)
+            update[span, :] = (rhs[1, span, :].astype(jnp.float32) - coupled).astype(jnp.bfloat16)
+        each(lines, lambda z0: solve(1, z0))
 
     sent = lambda copy: copy.wait_send()
 
-    turning(sent)
+    each(4, turning(sent))
 
     def sends(s):
         own_sends(s, sent)
@@ -325,7 +351,7 @@
     flops = 4 * order * order * samples
     return pl.pallas_call(
         functools.partial(kernel, stages, lines),
-        out_shape=jax.ShapeDtypeStruct(rhs.shape, jnp.float32),
+        out_shape=jax.ShapeDtypeStruct(rhs.shape, jnp.bfloat16),
         in_specs=[pl.BlockSpec(memory_space=pl.ANY)] * 4,
         out_specs=pl.BlockSpec(memory_space=pl.ANY),
         scratch_shapes=[
@@ -333,7 +359,7 @@
             pltpu.VMEM((2, order, half), jnp.bfloat16),
             pltpu.VMEM((3, order, half), jnp.bfloat16),
             pltpu.VMEM((order, half), jnp.bfloat16),
-            pltpu.VMEM((2, order, half), jnp.float32),
+            pltpu.VMEM((order, half), jnp.float32),
             pltpu.SemaphoreType.DMA((2,)),
             pltpu.SemaphoreType.DMA((3,)),
             pltpu.SemaphoreType.DMA((3,)),
@@ -351,7 +377,7 @@
         compiler_params=pltpu.CompilerParams(
             collective_id=0, has_side_effects=True, vmem_limit_bytes=60 * 1024 * 1024),
         cost_estimate=pl.CostEstimate(flops=flops, bytes_accessed=10 * order * samples, transcendentals=0),
-    )(inv_diag, sub_diag, rhs, carry_in)
+    )(inv_diag, sub_diag, rhs, carry_in).astype(jnp.float32)
 
 
 def solution(mesh):

time: 183 us -> 174 us (0.951); the launches traced: 182 us -> 171 us
  Pallas kernels: 178 us -> 167 us
  local copies, waits for them, and re-layouts: 4.64 us -> 0 us
  other arithmetic: 0 us -> 4.2 us
    pallas_call x1, Pallas kernels: 178 us -> 167 us  [shards(): pl.pallas_call(functools.partial(kernel, stages, lines), out_shape=jax.Sh...]
    unnamed x1 -> x0, local copies, waits for them, and re-layouts: 4.64 us -> none
    convert_element_type x0 -> x1, other arithmetic: none -> 4.2 us  [shards(): return pl.pallas_call(functools.partial(kernel, stages, lines), out_shape...]
where the time goes in v3:
time: 174 us; the launch traced here: 171 us
  Pallas kernels  167 us (96%)
  other arithmetic  4.2 us (2%)
    pallas_call x1, Pallas kernels, shards(): pl.pallas_call(functools.partial(kernel, stages, lines), out_shape=jax.Sh...  167 us
    convert_element_type x1, other arithmetic, shards(): return pl.pallas_call(functools.partial(kernel, stages, lines), out_shape...  4.2 us

profile of v3, /device:TPU:3, one launch (start us, length us, event | category | flops | bytes accessed | tf_op | source)
XLA Modules:
  0.0 170.9 jit_solution(2464389306114436420)
XLA Ops:
  0.0 166.7 %shard_map.46 = bf16[1,2048,512]{2,1,0:T(8,128)(2,1)} custom-call(bf16[1,256,2048]{2,1,0:T(8,128)(2,1)} %inv_ref.1, bf16[1,256,2048]{2,1,0:T(8,128)(2,1)} %sub_ref.1, bf16[1,2048,512]{2,1,0:T(8,128)(2,1)} %rhs_ref.1, bf16[2048,512]{1,0:T(8,128)(2,1)} %carry_ref.1), custom_call_target="tpu_custom_call" | custom-call | flops 8589934592 | bytes 10485760 | tf_op jit(solution)/shard_map/pallas_call | solution.py:352
  166.7 4.2 %convert_element_type.3 = f32[1,2048,512]{2,1,0:T(8,128)} convert(bf16[1,2048,512]{2,1,0:T(8,128)(2,1)} %shard_map.46) | non-fusion elementwise | flops 1048576 | bytes 6291456 | tf_op jit(solution)/shard_map/convert_element_type | solution.py:380

commit v4 on v3

--- a/solution.py
+++ b/solution.py
@@ -14,10 +14,12 @@
 LAGM = 4
 LATE = 6
 AHEAD = 2
-LAST = 2
+LAST = 1
 END_LAG = 1
 BEHIND = 1
 TALL = 1024
+STEPS = 8
+WIDEN_MIB = 60
 
 
 def kernel(stages, lines, inv_ref, sub_ref, rhs_ref, carry_ref, out_ref,
@@ -95,7 +97,9 @@
         return jnp.where(even(s), pieces, (c * rows) // WIDE + 1)
 
     def turns(s, c):
-        return jnp.where(s == 0, 1, jnp.where(s == 2, lax.rem(c, 2), 0))
+        z0, y0 = c // 2, lax.rem(c, 2)
+        third = jnp.where(z0 == 0, jnp.where(y0 == 1, pieces, 1), jnp.where(z0 == lines - 1, 0, y0))
+        return jnp.where(s == 0, 1, jnp.where(s == 2, third, jnp.where(jnp.logical_and(s == 3, z0 == 0), 1, 0)))
 
     def nth(s, c, k):
         return lax.rem(k + blocks(s, c) - turns(s, c), blocks(s, c))
@@ -256,6 +260,7 @@
     turning(start)(2)
     ready(1)
     ready(3)
+    turning(start)(3)
     own_rhs.wait()
     given_rhs(1 - core).wait_recv()
     if_(first, own_carry.wait)
@@ -301,6 +306,17 @@
         return carry
     lax.fori_loop(0, steps + max(LAG, LAGM, LATE) + BEHIND, step, 0)
 
+    sent = lambda copy: copy.wait_send()
+
+
+    def sends(s):
+        turning(sent)(s)
+        own_sends(s, sent)
+        turn(s, sent, False)
+        lax.fori_loop(1, lines, lambda d, carry: (relay(s, d, sent, False), carry)[1], 0)
+        each(lines, lambda z0: far(s, z0, sent, False))
+    if_(first, lambda: each(4, sends))
+
     @pl.when(stage > 0)
     def _():
         each(4, lambda s: each(lines, lambda z0: whole(s, z0)))
@@ -313,7 +329,11 @@
             for i in range(pieces):
                 span = pl.ds(i * WIDE, WIDE)
                 staged[span, :] -= jnp.dot(factors[0, span, group], prior[0, group, :], preferred_element_type=jnp.float32)
-        each(lines, lambda d: in_order(d, add))
+        for d in range(max(lines, 4)):
+            if d < 4:
+                sends(d)
+            if d < lines:
+                in_order(d, add)
         update[...] = staged[...].astype(jnp.bfloat16)
         each(lines, lambda z0: solve(0, z0))
         for i in range(order // TALL):
@@ -322,16 +342,6 @@
             update[span, :] = (rhs[1, span, :].astype(jnp.float32) - coupled).astype(jnp.bfloat16)
         each(lines, lambda z0: solve(1, z0))
 
-    sent = lambda copy: copy.wait_send()
-
-    each(4, turning(sent))
-
-    def sends(s):
-        own_sends(s, sent)
-        turn(s, sent, False)
-        lax.fori_loop(1, lines, lambda d, carry: (relay(s, d, sent, False), carry)[1], 0)
-        each(lines, lambda z0: far(s, z0, sent, False))
-    each(4, sends)
     for arr in range(2):
         given(arr, core).wait_send()
     given_rhs(core).wait_send()
@@ -345,11 +355,27 @@
     each(2 * lines, finish)
 
 
+def widen(in_ref, out_ref, narrow, wide, load_sem, store_sem):
+    rows = narrow.shape[0] // STEPS
+
+    spans = [pl.ds(i * rows, rows) for i in range(STEPS)]
+    loads = [pltpu.make_async_copy(in_ref.at[0, s, :], narrow.at[s, :], load_sem.at[i]) for i, s in enumerate(spans)]
+    stores = [pltpu.make_async_copy(wide.at[s, :], out_ref.at[0, s, :], store_sem.at[i]) for i, s in enumerate(spans)]
+    for load in loads:
+        load.start()
+    for span, load, store in zip(spans, loads, stores):
+        load.wait()
+        wide[span, :] = narrow[span, :].astype(jnp.float32)
+        store.start()
+    for store in stores:
+        store.wait()
+
+
 def shards(stages, cols, inv_diag, sub_diag, rhs, carry_in):
     order, samples = carry_in.shape
     half, lines, pieces = samples // 2, cols // 2, order // WIDE
     flops = 4 * order * order * samples
-    return pl.pallas_call(
+    result = pl.pallas_call(
         functools.partial(kernel, stages, lines),
         out_shape=jax.ShapeDtypeStruct(rhs.shape, jnp.bfloat16),
         in_specs=[pl.BlockSpec(memory_space=pl.ANY)] * 4,
@@ -377,7 +403,19 @@
         compiler_params=pltpu.CompilerParams(
             collective_id=0, has_side_effects=True, vmem_limit_bytes=60 * 1024 * 1024),
         cost_estimate=pl.CostEstimate(flops=flops, bytes_accessed=10 * order * samples, transcendentals=0),
-    )(inv_diag, sub_diag, rhs, carry_in).astype(jnp.float32)
+    )(inv_diag, sub_diag, rhs, carry_in)
+    return pl.pallas_call(
+        widen, in_specs=[pl.BlockSpec(memory_space=pl.ANY)], out_specs=pl.BlockSpec(memory_space=pl.ANY),
+        scratch_shapes=[
+            pltpu.VMEM((order, samples), jnp.bfloat16),
+            pltpu.VMEM((order, samples), jnp.float32),
+            pltpu.SemaphoreType.DMA((STEPS,)),
+            pltpu.SemaphoreType.DMA((STEPS,)),
+        ],
+        compiler_params=pltpu.CompilerParams(vmem_limit_bytes=WIDEN_MIB * 1024 * 1024),
+        out_shape=jax.ShapeDtypeStruct(rhs.shape, jnp.float32),
+        cost_estimate=pl.CostEstimate(flops=0, bytes_accessed=6 * order * samples, transcendentals=0),
+    )(result)
 
 
 def solution(mesh):

time: 174 us -> 169 us (0.971); the launches traced: 171 us -> 168 us
  other arithmetic: 4.2 us -> 0 us
    convert_element_type x1 -> x0, other arithmetic: 4.2 us -> none  [shards(): return pl.pallas_call(functools.partial(kernel, stages, lines), out_shape...]
    pallas_call x0 -> x1, Pallas kernels: none -> 3.12 us  [shards(): pl.pallas_call(widen, in_specs=[pl.BlockSpec(memory_space=pl.ANY)], out_s...]
    pallas_call x1, Pallas kernels: 167 us -> 165 us  [shards(): pl.pallas_call(functools.partial(kernel, stages, lines), out_shape=jax.Sh...]
where the time goes in v4:
time: 169 us; the launch traced here: 168 us
  Pallas kernels  168 us (99%)
    pallas_call x1, Pallas kernels, shards(): pl.pallas_call(functools.partial(kernel, stages, lines), out_shape=jax.Sh...  165 us

profile of v4, /device:TPU:3, one launch (start us, length us, event | category | flops | bytes accessed | tf_op | source)
XLA Modules:
  0.0 168.0 jit_solution(13500793860253568199)
XLA Ops:
  0.0 164.8 %shard_map.46.in_ref = bf16[1,2048,512]{2,1,0:T(8,128)(2,1)} custom-call(bf16[1,256,2048]{2,1,0:T(8,128)(2,1)} %inv_ref.1, bf16[1,256,2048]{2,1,0:T(8,128)(2,1)} %sub_ref.1, bf16[1,2048,512]{2,1,0:T(8,128)(2,1)} %rhs_ref.1, bf16[2048,512]{1,0:T(8,128)(2,1)} %carry_ref.1), custom_call_target="tpu_custom_call" | custom-call | flops 8589934592 | bytes 10485760 | tf_op jit(solution)/shard_map/pallas_call | solution.py:378
  164.8 3.1 %shard_map.47 = f32[1,2048,512]{2,1,0:T(8,128)} custom-call(bf16[1,2048,512]{2,1,0:T(8,128)(2,1)} %shard_map.46.in_ref), custom_call_target="tpu_custom_call" | custom-call | bytes 6291456 | tf_op jit(solution)/shard_map/pallas_call | solution.py:407

commit v5 on v4

--- a/solution.py
+++ b/solution.py
@@ -10,15 +10,16 @@
 MESH = pl.DeviceIdType.MESH
 WIDE = 512
 UP, DOWN, ACROSS, PAIR = 0, 1, 2, 3
-LAG = 4
-LAGM = 4
+LAG = 3
+LAGM = 3
 LATE = 6
-AHEAD = 2
-LAST = 1
+AHEAD = 1
+LAST = 2
 END_LAG = 1
 BEHIND = 1
 TALL = 1024
 STEPS = 8
+TURNS = [[[3, 0, 0, 0], [4, 0, 0, 0]], [[0, 0, 0, 0], [0, 0, 1, 0]], [[2, 0, 0, 2], [2, 0, 0, 4]], [[1, 0, 0, 0], [1, 0, 0, 0]]]
 WIDEN_MIB = 60
 
 
@@ -98,8 +99,10 @@
 
     def turns(s, c):
         z0, y0 = c // 2, lax.rem(c, 2)
-        third = jnp.where(z0 == 0, jnp.where(y0 == 1, pieces, 1), jnp.where(z0 == lines - 1, 0, y0))
-        return jnp.where(s == 0, 1, jnp.where(s == 2, third, jnp.where(jnp.logical_and(s == 3, z0 == 0), 1, 0)))
+        place = jnp.where(z0 == 0, 0, jnp.where(z0 == lines - 1, 3, jnp.where(z0 == 1, 1, 2))) + 4 * y0
+        packed = [sum(n << (3 * i) for i, n in enumerate(of[0] + of[1])) for of in TURNS]
+        of_stream = jnp.where(s == 0, packed[0], jnp.where(s == 1, packed[1], jnp.where(s == 2, packed[2], packed[3])))
+        return jnp.minimum(jnp.right_shift(of_stream, 3 * place) & 7, blocks(s, c))
 
     def nth(s, c, k):
         return lax.rem(k + blocks(s, c) - turns(s, c), blocks(s, c))
@@ -259,6 +262,7 @@
     ready(2)
     turning(start)(2)
     ready(1)
+    turning(start)(1)
     ready(3)
     turning(start)(3)
     own_rhs.wait()

time: 169 us -> 166 us (0.982)
  Pallas kernels: 168 us -> 166 us
    pallas_call x1, Pallas kernels: 165 us -> 163 us  [shards(): pl.pallas_call(functools.partial(kernel, stages, lines), out_shape=jax.Sh...]
where the time goes in v5:
time: 166 us
  Pallas kernels  166 us (100%)
    pallas_call x1, Pallas kernels, shards(): pl.pallas_call(functools.partial(kernel, stages, lines), out_shape=jax.Sh...  163 us

profile of v5, /device:TPU:3, one launch (start us, length us, event | category | flops | bytes accessed | tf_op | source)
XLA Modules:
  0.0 166.1 jit_solution(3056148557407692453)
XLA Ops:
  0.0 163.0 %shard_map.46.in_ref = bf16[1,2048,512]{2,1,0:T(8,128)(2,1)} custom-call(bf16[1,256,2048]{2,1,0:T(8,128)(2,1)} %inv_ref.1, bf16[1,256,2048]{2,1,0:T(8,128)(2,1)} %sub_ref.1, bf16[1,2048,512]{2,1,0:T(8,128)(2,1)} %rhs_ref.1, bf16[2048,512]{1,0:T(8,128)(2,1)} %carry_ref.1), custom_call_target="tpu_custom_call" | custom-call | flops 8589934592 | bytes 10485760 | tf_op jit(solution)/shard_map/pallas_call | solution.py:382
  163.0 3.1 %shard_map.47 = f32[1,2048,512]{2,1,0:T(8,128)} custom-call(bf16[1,2048,512]{2,1,0:T(8,128)(2,1)} %shard_map.46.in_ref), custom_call_target="tpu_custom_call" | custom-call | bytes 6291456 | tf_op jit(solution)/shard_map/pallas_call | solution.py:411

commit v6 on v5

--- a/solution.py
+++ b/solution.py
@@ -19,7 +19,7 @@
 BEHIND = 1
 TALL = 1024
 STEPS = 8
-TURNS = [[[3, 0, 0, 0], [4, 0, 0, 0]], [[0, 0, 0, 0], [0, 0, 1, 0]], [[2, 0, 0, 2], [2, 0, 0, 4]], [[1, 0, 0, 0], [1, 0, 0, 0]]]
+TURNS = [[[3, 0, 0, 0], [4, 0, 0, 0]], [[0, 0, 0, 0], [0, 0, 0, 0]], [[2, 0, 0, 2], [3, 0, 0, 3]], [[1, 0, 0, 0], [1, 0, 0, 0]]]
 WIDEN_MIB = 60
 
 

time: 166 us -> 169 us (1.018)
  Pallas kernels: 166 us -> 169 us
    pallas_call x1, Pallas kernels: 163 us -> 166 us  [shards(): pl.pallas_call(functools.partial(kernel, stages, lines), out_shape=jax.Sh...]
where the time goes in v6:
time: 169 us
  Pallas kernels  169 us (100%)
    pallas_call x1, Pallas kernels, shards(): pl.pallas_call(functools.partial(kernel, stages, lines), out_shape=jax.Sh...  166 us

profile of v6, /device:TPU:3, one launch (start us, length us, event | category | flops | bytes accessed | tf_op | source)
XLA Modules:
  0.0 169.3 jit_solution(13691605044837281971)
XLA Ops:
  0.0 166.2 %shard_map.46.in_ref = bf16[1,2048,512]{2,1,0:T(8,128)(2,1)} custom-call(bf16[1,256,2048]{2,1,0:T(8,128)(2,1)} %inv_ref.1, bf16[1,256,2048]{2,1,0:T(8,128)(2,1)} %sub_ref.1, bf16[1,2048,512]{2,1,0:T(8,128)(2,1)} %rhs_ref.1, bf16[2048,512]{1,0:T(8,128)(2,1)} %carry_ref.1), custom_call_target="tpu_custom_call" | custom-call | flops 8589934592 | bytes 10485760 | tf_op jit(solution)/shard_map/pallas_call | solution.py:382
  166.2 3.1 %shard_map.47 = f32[1,2048,512]{2,1,0:T(8,128)} custom-call(bf16[1,2048,512]{2,1,0:T(8,128)(2,1)} %shard_map.46.in_ref), custom_call_target="tpu_custom_call" | custom-call | bytes 6291456 | tf_op jit(solution)/shard_map/pallas_call | solution.py:411
